TPU v7x, 32 devices: a whole 2x2x4 slice. The times are simulated.
32 devices in a mesh: ctx: 8 (over z, y), head: 4 (over x, core).
Axes of the slice: x: 2, y: 2, z: 4, core: 2. Of those that a mesh axis runs over, the one named last changes fastest.
Arguments:
- prompt_states: bfloat16 [4096, 2048], P('ctx')
- decode_states: bfloat16 [4, 2048], replicated
- lengths: int32 [4], replicated, may hold values from 1 to 2048, 4096 in all
- page_table: int32 [32], replicated, may hold values from 0 to 31, as said below
- w_query: bfloat16 [2048, 3072], P(None, 'head'), may hold values from -0.125 to 0.125
- w_down: bfloat16 [2048, 576], replicated, may hold values from -0.125 to 0.125
- kv_gain: float32 [512], replicated, may hold values from 0.1 to 1.9
- w_up: bfloat16 [512, 4096], P(None, 'head'), may hold values from -0.25 to 0.25
- w_out: bfloat16 [2048, 2048], P('head'), may hold values from -0.125 to 0.125
Outputs:
- prefill_out: bfloat16 [4096, 2048], P(('ctx', 'head'))
- paged_cache: bfloat16 [4096, 576], P('ctx')
- decode_out: bfloat16 [4, 2048], replicated
Inputs may be any that keep to these rules, and one draw needn't show every extreme that they name: page_table is a permutation of the 32 pages; the logical pages of ctx index c are c * 4 to c * 4 + 3, and physical page p lies on ctx index p // 4; logical page c * 4 + w has physical page ((c + s_w) mod 8) * 4 + w, where the shifts s_0 to s_(3) are distinct numbers of 0 to 8 - 1, the same for every c.
All inputs are finite; a program needn't handle non-finite values.
Results may differ from a plain program's by a relative error of at most 0.025.
Values may be sent and summed in bfloat16 or wider, within the bound.
A program may use at most 192 MiB of HBM per device.

v0:
```python
import jax
import jax.numpy as jnp
from jax import lax
from jax.sharding import PartitionSpec as P

NOPE = 128
ROPE = 64
VDIM = 128
RANK = 512
PAGE = 128


ROPE_BASE = 50000.0
FAR_LOW = -1e30


def from_behind(block, axis, distance):
    devices = range(lax.axis_size(axis))
    route = [((i - distance) % len(devices), i) for i in devices]
    return lax.ppermute(block, axis, route)


def combined_all(value, axis, join):
    pieces = jax.tree.map(lambda part: lax.all_gather(part, axis), value)
    head = jax.tree.map(lambda part: part[0], pieces)
    tail = jax.tree.map(lambda part: part[1:], pieces)
    subtotal, _ = lax.scan(lambda subtotal, piece: (join(subtotal, piece), None), head, tail)
    return subtotal


def rope(vector, place):
    half = vector.shape[-1] // 2
    freq = ROPE_BASE ** (-(jnp.arange(half, dtype=jnp.float32) * 2.0 / vector.shape[-1]))
    angle = place[..., None] * freq
    first, second = (vector[..., :half], vector[..., half:])
    return jnp.concatenate(
        [
            first * jnp.cos(angle) - second * jnp.sin(angle),
            first * jnp.sin(angle) + second * jnp.cos(angle),
        ],
        -1,
    )


def token_info(index, lengths):
    ends = jnp.cumsum(lengths)
    starts = ends - lengths
    tenant = jnp.sum((index[:, None] >= ends[None, :]).astype(jnp.int32), 1)
    picked = jnp.sum(
        jnp.where(
            tenant[:, None] == jnp.arange(lengths.shape[0], dtype=jnp.int32)[None, :],
            starts[None, :],
            0,
        ),
        1,
    )
    return (tenant, index - picked)


def latent_of(states, w_down, kv_gain, place):
    lat = jnp.dot(states, w_down, preferred_element_type=jnp.float32)
    comp = lat[:, :RANK]
    comp = comp * lax.rsqrt(jnp.mean(comp * comp, -1, keepdims=True) + 1e-06) * kv_gain
    return jnp.concatenate([comp, rope(lat[:, RANK:], place)], 1).astype(jnp.bfloat16)


def queries(states, w_query, w_up, place):
    rows = states.shape[0]
    heads = w_query.shape[1] // (NOPE + ROPE)
    qfull = (
        jnp.dot(states, w_query, preferred_element_type=jnp.float32)
        .astype(jnp.bfloat16)
        .reshape(rows, heads, NOPE + ROPE)
    )
    w_key = w_up.reshape(RANK, heads, NOPE + VDIM)[:, :, :NOPE]
    qnope = jnp.einsum("thn,rhn->thr", qfull[..., :NOPE], w_key, preferred_element_type=jnp.float32)
    qrope = rope(qfull[..., NOPE:].astype(jnp.float32), place[:, None])
    scale = (NOPE + ROPE) ** (-0.5)
    return (jnp.concatenate([qnope, qrope], -1) * scale).astype(jnp.bfloat16)


def values_of(mixed, w_up):
    heads = w_up.shape[1] // (NOPE + VDIM)
    w_val = w_up.reshape(RANK, heads, NOPE + VDIM)[:, :, NOPE:]
    out = jnp.einsum("thr,rhv->thv", mixed, w_val, preferred_element_type=jnp.float32)
    return out.astype(jnp.bfloat16).reshape(mixed.shape[0], heads * VDIM)


def combine_parts(first, second):
    top = jnp.maximum(first[0], second[0])
    ratio_a = jnp.exp(first[0] - top)
    ratio_b = jnp.exp(second[0] - top)
    return (
        top,
        first[1] * ratio_a + second[1] * ratio_b,
        first[2] * ratio_a[..., None] + second[2] * ratio_b[..., None],
    )


def on_device(
    prompt_states, decode_states, lengths, page_table, w_query, w_down, kv_gain, w_up, w_out
):
    tok = prompt_states.shape[0]
    width = RANK + ROPE
    ctx_pos = lax.axis_index("ctx")
    ctx_count = lax.axis_size("ctx")
    index = ctx_pos * tok + jnp.arange(tok, dtype=jnp.int32)
    tenant, place = token_info(index, lengths)
    latent = latent_of(prompt_states, w_down, kv_gain, place.astype(jnp.float32))
    query = queries(prompt_states, w_query, w_up, place.astype(jnp.float32))
    heads = query.shape[1]
    pages_dev = tok // PAGE
    total_pages = page_table.shape[0]
    physical = ctx_pos * pages_dev + jnp.arange(pages_dev, dtype=jnp.int32)
    owned = jnp.sum(
        jnp.where(
            page_table[None, :] == physical[:, None],
            jnp.arange(total_pages, dtype=jnp.int32)[None, :],
            0,
        ),
        1,
    )
    slot_rows = (owned[:, None] * PAGE + jnp.arange(PAGE, dtype=jnp.int32)[None, :]).reshape(-1)
    piece = lax.all_gather(latent, "ctx", axis=0, tiled=True)
    top = jnp.full((tok, heads), FAR_LOW, jnp.float32)
    count = piece.shape[0]
    key_index = jnp.arange(count, dtype=jnp.int32)
    key_tenant, unused = token_info(key_index, lengths)
    mask = (key_tenant[None, :] == tenant[:, None]) & (key_index[None, :] <= index[:, None])
    score = jnp.einsum("thk,ck->thc", query, piece, preferred_element_type=jnp.float32)
    score = jnp.where(mask[:, None, :], score, FAR_LOW)
    new_top = jnp.maximum(top, jnp.max(score, -1))
    prob = jnp.where(mask[:, None, :], jnp.exp(score - new_top[..., None]), 0.0)
    new_total = jnp.sum(prob, -1)
    new_acc = jnp.einsum(
        "thc,cr->thr",
        prob.astype(jnp.bfloat16),
        piece[:, :RANK],
        preferred_element_type=jnp.float32,
    )
    mixed = (new_acc / new_total[..., None]).astype(jnp.bfloat16)
    heads_out = values_of(mixed, w_up)
    prefill_out = lax.psum_scatter(
        jnp.dot(heads_out, w_out, preferred_element_type=jnp.float32).astype(jnp.bfloat16),
        "head",
        scatter_dimension=0,
        tiled=True,
    )
    shifts = page_table[:pages_dev] // pages_dev
    stacked = latent.reshape(pages_dev, PAGE, width)
    for bit in range((ctx_count - 1).bit_length()):
        moved = from_behind(stacked, "ctx", 1 << bit)
        chosen = shifts // (1 << bit) % 2 == 1
        stacked = jnp.where(chosen[:, None, None], moved, stacked)
    paged_cache = stacked.reshape(pages_dev * PAGE, width)
    requests = decode_states.shape[0]
    dplace = lengths.astype(jnp.float32)
    new_key = latent_of(decode_states, w_down, kv_gain, dplace)
    dquery = queries(decode_states, w_query, w_up, dplace)
    key_tenant, unused = token_info(slot_rows, lengths)
    dmask = key_tenant[None, :] == jnp.arange(requests, dtype=jnp.int32)[:, None]
    score = jnp.einsum("qhk,ck->qhc", dquery, paged_cache, preferred_element_type=jnp.float32)
    score = jnp.where(dmask[:, None, :], score, FAR_LOW)
    top = jnp.max(score, -1)
    prob = jnp.where(dmask[:, None, :], jnp.exp(score - top[..., None]), 0.0)
    total = jnp.sum(prob, -1)
    acc = jnp.einsum(
        "qhc,cr->qhr",
        prob.astype(jnp.bfloat16),
        paged_cache[:, :RANK],
        preferred_element_type=jnp.float32,
    )
    top, total, acc = combined_all((top, total, acc), "ctx", combine_parts)
    own = jnp.einsum("qhk,qk->qh", dquery, new_key, preferred_element_type=jnp.float32)
    best = jnp.maximum(top, own)
    ratio = jnp.exp(top - best)
    pown = jnp.exp(own - best)
    total = total * ratio + pown
    acc = acc * ratio[..., None] + pown.astype(jnp.bfloat16).astype(jnp.float32)[
        ..., None
    ] * new_key[:, None, :RANK].astype(jnp.float32)
    dmixed = (acc / total[..., None]).astype(jnp.bfloat16)
    dheads = values_of(dmixed, w_up)
    partial_out = jnp.dot(dheads, w_out, preferred_element_type=jnp.float32)
    decode_out = lax.psum(partial_out.astype(jnp.bfloat16), "head")
    return (prefill_out, paged_cache, decode_out)


def solution(mesh):
    in_specs = (
        P("ctx", None),
        P(),
        P(),
        P(),
        P(None, "head"),
        P(),
        P(),
        P(None, "head"),
        P("head", None),
    )
    out_specs = (P(("ctx", "head"), None), P("ctx", None), P())
    return jax.shard_map(
        on_device, mesh=mesh, in_specs=in_specs, out_specs=out_specs, check_vma=False
    )
```

profile of v0, /device:TPU:17, one launch (start us, length us, event | category | flops | bytes accessed | tf_op | source)
XLA Modules:
  0.0 304.2 jit_solution(9261015198521083043)
XLA Ops:
  7.3 1.0 select_reduce_fusion.2
  8.3 0.8 reduce-window.8
  9.2 0.7 fusion.60
  10.1 3.7 %fusion.62 = f32[512,576]{0,1:T(8,128)S(1)} fusion(bf16[512,2048]{1,0:T(8,128)(2,1)} %param.11, bf16[2048,576]{0,1:T(8,128)(2,1)} %param.16), kind=kOutput, calls=%fused_computation.141 | convolution fusion | flops 1207959552 | bytes 5636096 | tf_op jit(solution)/shard_map/dot_general | solution.py:61
  14.5 0.8 copy-done.5
  15.3 0.9 pad_maximum_fusion
  16.2 2.0 concatenate.26
  18.2 2.0 constant_dynamic-update-slice_fusion.2
  20.2 0.6 constant_dynamic-update-slice_fusion.1
  20.8 0.6 constant_dynamic-update-slice_fusion
  21.4 1.2 collective-permute-start
  22.7 0.5 convolution_convert_fusion.3
  23.3 4.3 %convolution_convert_fusion.2 = bf16[512,768]{1,0:T(8,128)(2,1)} fusion(bf16[512,2048]{1,0:T(8,128)(2,1)} %param.11, bf16[2048,768]{1,0:T(8,128)(2,1)S(1)} %copy-done), kind=kOutput, calls=%fused_computation.27 | convolution fusion | flops 1611005952 | bytes 6029312 | tf_op jit(solution)/shard_map/dot_general | solution.py:71
  27.6 2.4 copy.58
  29.9 1.5 copy.60
  31.5 2.8 fusion.63
  34.8 2.7 fusion.8
  37.8 5.5 %collective-permute-done = bf16[4,128,576]{1,0,2:T(4,128)(2,1)} collective-permute-done((bf16[4,128,576]{1,0,2:T(4,128)(2,1)}, bf16[4,128,576]{1,0,2:T(4,128)(2,1)}, u32[]{:S(2)}, u32[]{:S(2)}) %collective-permute-start) | collective-permute-done | bytes 589856 | tf_op jit(solution)/shard_map/ppermute | solution.py:20
  43.2 1.6 broadcast_select_fusion
  44.9 1.3 collective-permute-start.1
  46.3 0.9 multiply_subtract_fusion
  47.2 13.7 %collective-permute-done.1 = bf16[4,128,576]{1,0,2:T(4,128)(2,1)S(1)} collective-permute-done((bf16[4,128,576]{1,0,2:T(4,128)(2,1)S(1)}, bf16[4,128,576]{1,0,2:T(4,128)(2,1)S(1)}, u32[]{:S(2)}, u32[]{:S(2)}) %collective-permute-start.1) | collective-permute-done | bytes 589856 | tf_op jit(solution)/shard_map/ppermute | solution.py:20
  60.9 0.4 broadcast_select_fusion.1
  61.3 8.8 %collective-permute-start.2 = (bf16[4,128,576]{1,0,2:T(4,128)(2,1)S(1)}, bf16[4,128,576]{1,0,2:T(4,128)(2,1)S(1)}, u32[]{:S(2)}, u32[]{:S(2)}) collective-permute-start(bf16[4,128,576]{1,0,2:T(4,128)(2,1)S(1)} %broadcast_select_fusion.1), channel_id=1, source_target_pairs={{16,0},{20,4},{24,8},{28,12},{0,16},{4,20},{8,24},{12,28},{17,1},{... | collective-permute-start | bytes 1769480 | tf_op jit(solution)/shard_map/ppermute | solution.py:20
  70.3 2.8 convolution_bitcast_fusion
  73.1 42.2 %collective-permute-done.2 = bf16[4,128,576]{1,0,2:T(4,128)(2,1)S(1)} collective-permute-done((bf16[4,128,576]{1,0,2:T(4,128)(2,1)S(1)}, bf16[4,128,576]{1,0,2:T(4,128)(2,1)S(1)}, u32[]{:S(2)}, u32[]{:S(2)}) %collective-permute-start.2) | collective-permute-done | bytes 589856 | tf_op jit(solution)/shard_map/ppermute | solution.py:20
  115.2 1.2 broadcast_select_fusion.2
  116.4 1.6 copy.63
  118.0 0.4 fusion.61
  118.4 30.9 %all-gather.3 = f32[8,4,4]{2,1,0:T(4,128)S(1)} all-gather(f32[1,4,4]{2,1,0:T(4,128)S(1)} %bitcast.96), channel_id=2, replica_groups=mesh['ctx'=8,'head'=4] {'ctx'}, dimensions={0}, use_global_device_ids=true | all-gather | bytes 576 | tf_op jit(solution)/shard_map/all_gather | solution.py:24
  149.7 23.5 %select_reduce_fusion = (f32[512,4]{0,1:T(4,128)S(1)}, f32[512,4,4096]{2,0,1:T(8,128)}) fusion(pred[512,4096]{1,0:T(8,128)(4,1)S(1)} %fusion.8, bf16[4096,576]{0,1:T(8,128)(2,1)} %all-gather.7.cloned.1.call-done, f32[512,4,32]{0,2,1:T(8,128)S(1)} %copy-done.8, f32[512,4,32]{0,2,1:T(8,128)S(1)} %copy-done.7, f32[512,4,512]{0,2,1:T(8,128)} %convolution_bitcast_fusion), kind=kOutput, calls=%fused_computation.9 | convolution fusion | flops 9685170176 | bytes 45096960 | tf_op jit(solution)/shard_map/thk,ck->thc/dot_general | solution.py:130
  173.3 15.3 %fusion.3 = f32[512,4]{0,1:T(4,128)S(1)} fusion(f32[512,4,4096]{2,0,1:T(8,128)} %get-tuple-element.106, f32[512,4]{0,1:T(4,128)S(1)} %broadcast_maximum_fusion, pred[512,4096]{1,0:T(8,128)(4,1)S(1)} %fusion.8), kind=kLoop, calls=%fused_computation.10 | loop fusion | flops 33552384 | bytes 35667968 | tf_op jit(solution)/shard_map/reduce_sum | solution.py:134
  188.6 17.8 %fusion.15 = bf16[4,512,128]{1,2,0:T(8,128)(2,1)} fusion(f32[512,4]{0,1:T(4,128)S(1)} %fusion.3, bf16[512,4,256]{0,2,1:T(8,128)(2,1)S(1)} %bitcast.92, f32[512,4,4096]{2,0,1:T(8,128)} %get-tuple-element.106, f32[512,4]{0,1:T(4,128)S(1)} %broadcast_maximum_fusion, pred[512,4096]{1,0:T(8,128)(4,1)S(1)} %fusion.8, ...), kind=kOutput, calls=%fused_computation.28 | convolution fusion | flops 8894283776 | bytes 40910848 | tf_op jit(solution)/shard_map/thr,rhv->thv/dot_general | solution.py:85
  206.4 4.5 %convolution_convert_fusion = bf16[512,2048]{1,0:T(8,128)(2,1)} fusion(bf16[512,512]{0,1:T(8,128)(2,1)} %bitcast.102, bf16[512,2048]{1,0:T(8,128)(2,1)} %param.19), kind=kOutput, calls=%fused_computation.22 | convolution fusion | flops 1074790400 | bytes 4718592 | tf_op jit(solution)/shard_map/dot_general | solution.py:144
  211.0 23.5 %all-gather.2 = f32[32,4,512]{2,1,0:T(4,128)S(1)} all-gather(f32[4,4,512]{2,1,0:T(4,128)S(1)} %fusion.17), channel_id=4, replica_groups=mesh['ctx'=8,'head'=4] {'ctx'}, dimensions={0}, use_global_device_ids=true | all-gather | bytes 294912 | tf_op jit(solution)/shard_map/all_gather | solution.py:24
  234.5 2.1 copy.70
  236.6 0.7 slice.142
  237.3 22.5 %all-gather.4 = f32[8,4,4]{2,1,0:T(4,128)S(1)} all-gather(f32[1,4,4]{2,1,0:T(4,128)S(1)} %bitcast.97), channel_id=3, replica_groups=mesh['ctx'=8,'head'=4] {'ctx'}, dimensions={0}, use_global_device_ids=true | all-gather | bytes 576 | tf_op jit(solution)/shard_map/all_gather | solution.py:24
  259.9 6.2 %while.14 = (s32[]{:T(128)}, f32[4,4]{1,0:T(4,128)S(1)}, f32[4,4]{1,0:T(4,128)S(1)}, f32[4,4,512]{2,1,0:T(4,128)S(1)}, f32[7,4,4]{2,1,0:T(4,128)S(1)}, /*index=5...) while((s32[]{:T(128)}, f32[4,4]{1,0:T(4,128)S(1)}, f32[4,4]{1,0:T(4,128)S(1)}, ...), condition=%wide.region_13.14_spmd, body=%wide.region_12.13_spmd.sunk | while | flops 24674 | bytes 99045 | solution.py:27
  259.9 0.8 fusion.79
  260.8 0.8 fusion.79
  261.7 0.8 fusion.79
  262.6 0.8 fusion.79
  263.5 0.8 fusion.79
  264.4 0.8 fusion.79
  265.3 0.8 fusion.79
  266.2 2.3 convolution_convert_fusion.1
  268.6 28.8 %psum.7 = bf16[4,2048]{1,0:T(4,128)(2,1)} all-reduce(bf16[4,2048]{1,0:T(4,128)(2,1)S(1)} %convolution_convert_fusion.1), channel_id=1, replica_groups=mesh['ctx'=8,'head'=4] {'head'}, use_global_device_ids=true, to_apply=%region_15.16 | all-reduce | flops 8192 | bytes 32768 | tf_op jit(solution)/shard_map/psum | solution.py:185
  (82 shorter events, 3.0 us)
Async XLA Ops:
  7.2 15.5 %copy-start = (bf16[2048,768]{1,0:T(8,128)(2,1)S(1)}, bf16[2048,768]{1,0:T(8,128)(2,1)}, u32[]{:S(2)}) copy-start(bf16[2048,768]{1,0:T(8,128)(2,1)} %param.15) | copy-start | bytes 9437188
  7.2 142.5 %all-gather.7.cloned.1.call-start = ((), (), s32[]{:S(2)}) async-start(), calls=%async_computation.1 | async-start | bytes 5308416 | tf_op jit(solution)/shard_map/all_gather | solution.py:124
  10.1 4.2 %copy-start.11 = (f32[512]{0:T(512)S(1)}, f32[512]{0:T(512)}, u32[]{:S(2)}) copy-start(f32[512]{0:T(512)} %param.17) | copy-start | bytes 6148
  13.8 8.9 %copy-start.9 = (bf16[4,2048]{1,0:T(4,128)(2,1)S(1)}, bf16[4,2048]{1,0:T(4,128)(2,1)}, u32[]{:S(2)}) copy-start(bf16[4,2048]{1,0:T(4,128)(2,1)} %param.12) | copy-start | bytes 49156
  14.5 0.8 copy-start.5
  16.1 281.2 %reduce-scatter.2.cloned.1.call-start = ((), (), s32[]{:S(2)}) async-start(), calls=%async_computation.2 | async-start | bytes 2621440 | tf_op jit(solution)/shard_map/reduce_scatter | solution.py:143
  21.4 21.8 %collective-permute-start = (bf16[4,128,576]{1,0,2:T(4,128)(2,1)}, bf16[4,128,576]{1,0,2:T(4,128)(2,1)}, u32[]{:S(2)}, u32[]{:S(2)}) collective-permute-start(bf16[4,128,576]{1,0,2:T(4,128)(2,1)} %constant_dynamic-update-slice_fusion), channel_id=1, source_target_pairs={{28,0},{0,4},{4,8},{8,12},{12,16},{16,20},{20,24},{24,28},{29,1},{... | collective-permute-start | bytes 1769480 | tf_op jit(solution)/shard_map/ppermute | solution.py:20
  23.3 4.3 %copy-start.10 = (bf16[4,4,192]{2,1,0:T(4,128)(2,1)}, bf16[4,4,192]{2,1,0:T(4,128)(2,1)S(1)}, u32[]{:S(2)}) copy-start(bf16[4,4,192]{2,1,0:T(4,128)(2,1)S(1)} %reshape.320) | copy-start | bytes 18436
  27.6 7.0 %copy-start.12 = (s32[32]{0:T(128)S(1)}, s32[32]{0:T(128)}, u32[]{:S(2)}) copy-start(s32[32]{0:T(128)} %param.14) | copy-start | bytes 388
  29.9 4.8 %slice-start = ((bf16[4,4,192]{2,1,0:T(4,128)(2,1)}), bf16[4,4,64]{2,1,0:T(4,128)(2,1)S(1)}, s32[]{:S(2)}) async-start(bf16[4,4,192]{2,1,0:T(4,128)(2,1)} %copy-done.10), calls=%async_computation.3 | async-start | bytes 8192 | tf_op jit(solution)/shard_map/slice | solution.py:77
  29.9 7.6 %slice-start.1 = ((bf16[4,4,192]{2,1,0:T(4,128)(2,1)}), bf16[4,4,128]{2,1,0:T(4,128)(2,1)S(1)}, s32[]{:S(2)}) async-start(bf16[4,4,192]{2,1,0:T(4,128)(2,1)} %copy-done.10), calls=%async_computation.4 | async-start | bytes 8192 | tf_op jit(solution)/shard_map/slice | solution.py:76
  31.5 38.8 %copy-start.3 = (bf16[512,1024]{0,1:T(8,128)(2,1)}, bf16[512,1024]{0,1:T(8,128)(2,1)S(1)}, u32[]{:S(2)}) copy-start(bf16[512,1024]{0,1:T(8,128)(2,1)S(1)} %copy.60) | copy-start | bytes 3145732
  31.5 14.8 %copy-start.6 = (bf16[512,768]{0,1:T(8,128)(2,1)S(1)}, bf16[512,768]{0,1:T(8,128)(2,1)}, u32[]{:S(2)}) copy-start(bf16[512,768]{0,1:T(8,128)(2,1)} %copy.58) | copy-start | bytes 2359300
  44.9 16.0 %collective-permute-start.1 = (bf16[4,128,576]{1,0,2:T(4,128)(2,1)S(1)}, bf16[4,128,576]{1,0,2:T(4,128)(2,1)S(1)}, u32[]{:S(2)}, u32[]{:S(2)}) collective-permute-start(bf16[4,128,576]{1,0,2:T(4,128)(2,1)S(1)} %broadcast_select_fusion), channel_id=1, source_target_pairs={{24,0},{28,4},{0,8},{4,12},{8,16},{12,20},{16,24},{20,28},{25,1},{... | collective-permute-start | bytes 1769480 | tf_op jit(solution)/shard_map/ppermute | solution.py:20
  61.3 54.0 %collective-permute-start.2 = (bf16[4,128,576]{1,0,2:T(4,128)(2,1)S(1)}, bf16[4,128,576]{1,0,2:T(4,128)(2,1)S(1)}, u32[]{:S(2)}, u32[]{:S(2)}) collective-permute-start(bf16[4,128,576]{1,0,2:T(4,128)(2,1)S(1)} %broadcast_select_fusion.1), channel_id=1, source_target_pairs={{16,0},{20,4},{24,8},{28,12},{0,16},{4,20},{8,24},{12,28},{17,1},{... | collective-permute-start | bytes 1769480 | tf_op jit(solution)/shard_map/ppermute | solution.py:20
  70.3 79.4 %copy-start.7 = (f32[512,4,32]{0,2,1:T(8,128)S(1)}, f32[512,4,32]{0,2,1:T(8,128)}, u32[]{:S(2)}) copy-start(f32[512,4,32]{0,2,1:T(8,128)} %get-tuple-element.88) | copy-start | bytes 786436
  73.1 76.6 %copy-start.8 = (f32[512,4,32]{0,2,1:T(8,128)S(1)}, f32[512,4,32]{0,2,1:T(8,128)}, u32[]{:S(2)}) copy-start(f32[512,4,32]{0,2,1:T(8,128)} %get-tuple-element.89) | copy-start | bytes 786436
  118.0 55.3 %copy-start.2 = (bf16[4,128,576]{2,1,0:T(8,128)(2,1)}, bf16[4,128,576]{2,1,0:T(8,128)(2,1)S(1)}, u32[]{:S(2)}) copy-start(bf16[4,128,576]{2,1,0:T(8,128)(2,1)S(1)} %copy.63) | copy-start | bytes 1769476
  173.3 15.3 %copy-start.4 = (bf16[512,1024]{0,1:T(8,128)(2,1)S(1)}, bf16[512,1024]{0,1:T(8,128)(2,1)}, u32[]{:S(2)}) copy-start(bf16[512,1024]{0,1:T(8,128)(2,1)} %copy-done.3) | copy-start | bytes 3145732
  206.4 91.0 %copy-start.1 = (bf16[2048,768]{1,0:T(8,128)(2,1)S(1)}, bf16[2048,768]{1,0:T(8,128)(2,1)}, u32[]{:S(2)}) copy-start(bf16[2048,768]{1,0:T(8,128)(2,1)} %param.15) | copy-start | bytes 9437188
Sparse Core Ops, SparseCore 0:
  16.3 120.9 all-gather.6
  211.1 38.9 reduce-scatter.1
where the time goes:
time: 310 us; the launch traced here: 304 us
  blocking collectives  106 us (34%)
  matrix products  63.2 us (20%)
  waiting for transfers between devices  61.4 us (20%)
  other arithmetic  33.5 us (11%)
  local copies, waits for them, and re-layouts  14.5 us (5%)
  between operations  14.4 us (5%)
  starting transfers between devices  11.5 us (4%)
    all_gather x3, blocking collectives, combined_all(): pieces = jax.tree.map(lambda part: lax.all_gather(part, axis), value)  76.9 us
    ppermute x3, waiting for transfers between devices, from_behind(): return lax.ppermute(block, axis, route)  61.3 us
    psum x1, blocking collectives, on_device(): decode_out = lax.psum(partial_out.astype(jnp.bfloat16), 'head')  28.8 us
    dot_general x1, matrix products, on_device(): jnp.einsum('thk,ck->thc', query, piece, preferred_element_type=jnp.float32)  23.5 us
    dot_general x1, matrix products, values_of(): jnp.einsum('thr,rhv->thv', mixed, w_val, preferred_element_type=jnp.float32)  17.8 us
    reduce_sum x1, other arithmetic, on_device(): new_total = jnp.sum(prob, -1)  15.3 us
    ppermute x3, starting transfers between devices, from_behind(): return lax.ppermute(block, axis, route)  11.4 us
    unnamed x30, local copies, waits for them, and re-layouts  7.12 us
  transfers between devices with their start and end apart: 5, of which 3 were waited for; matrix products, arithmetic and copies ran while one was open for 14% of the time, Pallas kernels for 0%

commit v1 on v0

v1 whole, which is shorter than its diff:
```python
import functools
import math

import jax
import jax.numpy as jnp
from jax import lax
from jax.experimental import pallas as pl
from jax.experimental.pallas import tpu as pltpu
from jax.sharding import PartitionSpec as P

NOPE = 128
ROPE = 64
VDIM = 128
RANK = 512
PAGE = 128
WIDTH = RANK + ROPE
QK = NOPE + ROPE
ROPE_BASE = 50000.0
NEG = -1e30
SCALE = QK ** (-0.5) * math.log2(math.e)
MESH = pl.DeviceIdType.MESH
LINE = 4


def trig(place, size):
    half = size // 2
    freq = ROPE_BASE ** (-(jnp.arange(half, dtype=jnp.float32) * 2.0 / size))
    angle = place[..., None] * freq
    return jnp.cos(angle), jnp.sin(angle)


def turn(vector, cos, sin):
    half = vector.shape[-1] // 2
    first, second = vector[..., :half], vector[..., half:]
    return jnp.concatenate([first * cos - second * sin, first * sin + second * cos], -1)


def latent_of(states, w_down, kv_gain, cos, sin):
    lat = jnp.dot(states, w_down, preferred_element_type=jnp.float32)
    comp = lat[:, :RANK]
    comp = comp * lax.rsqrt(jnp.mean(comp * comp, -1, keepdims=True) + 1e-06) * kv_gain
    return jnp.concatenate([comp, turn(lat[:, RANK:], cos, sin)], 1).astype(jnp.bfloat16)


def kernel(
    n_ctx, n_head, heads, q_ref, lat_ref, start_ref, dq_ref, dtop_ref, dacc_ref, dlow_ref, dhigh_ref,
    shift_ref, w_up_ref, w_out_ref, out_ref, cache_ref, dec_ref,
    got, kbuf, vbuf, acc, top, ho, sib_out, sib_in, far_out, far_in, near_out, near_in,
    dsib_out, dsib_in, dfar, send_sems, recv_sems, core_sems, sum_send, sum_recv,
):
    tok = lat_ref.shape[0]
    half = tok // 2
    line_b = n_ctx // LINE
    window = n_ctx // 2
    c = lax.axis_index("ctx")
    m = lax.axis_index("head")
    a, b = c // line_b, c % line_b
    x, k = m // 2, m % 2
    sib = x * 2 + 1 - k
    n_x = n_head // 2
    fars = [lax.rem(x + r, n_x) for r in range(1, n_x)]
    up_a, dn_a, up_b, dn_b = a < LINE - 1, a > 0, b < line_b - 1, b > 0
    moves = [(up_a, line_b), (dn_a, -line_b), (up_b, 1), (dn_b, -1)]

    barrier = pltpu.get_barrier_semaphore()
    for ok, step in moves:
        @pl.when(ok)
        def _(step=step):
            pl.semaphore_signal(barrier, inc=1, device_id=(c + step, m), device_id_type=MESH)
    for other in [sib] + [xo * 2 + k for xo in fars]:
        pl.semaphore_signal(barrier, inc=1, device_id=(c, other), device_id_type=MESH)
    peers = jnp.minimum(a, 1) + jnp.minimum(LINE - 1 - a, 1)
    peers = peers + jnp.minimum(b, 1) + jnp.minimum(line_b - 1 - b, 1)
    pl.semaphore_wait(barrier, peers + n_x)

    def hop(blk, way):
        return pltpu.make_async_remote_copy(
            src_ref=got.at[blk, k], dst_ref=got.at[blk, k], send_sem=send_sems.at[way, blk],
            recv_sem=recv_sems.at[blk], device_id=(c + moves[way][1], m), device_id_type=MESH)

    def across(blk, side):
        return pltpu.make_async_remote_copy(
            src_ref=got.at[blk, side], dst_ref=got.at[blk, side], send_sem=send_sems.at[4, blk],
            recv_sem=core_sems.at[blk], device_id=(c, sib), device_id_type=MESH)

    sent = []

    def send(ok, blk, way):
        @pl.when(ok)
        def _():
            (hop(blk, way) if way < 4 else across(blk, k)).start()
        sent.append((ok, blk, way))

    got[c] = lat_ref[...].reshape(2, half, WIDTH)
    for way in range(4):
        send(moves[way][0], c, way)

    far_step = LINE - 1 + line_b - 1
    stages = [[] for _ in range(far_step + 1)]
    for i in range(-(LINE - 1), LINE):
        for j in range(-(line_b - 1), line_b):
            if (i, j) != (0, 0):
                stages[abs(i) + abs(j)].append((i, j))

    def where_from(i, j):
        ok = jnp.logical_and(jnp.logical_and(a + i >= 0, a + i < LINE),
                             jnp.logical_and(b + j >= 0, b + j < line_b))
        blk = lax.rem(c + i * line_b + j + n_ctx * 2, n_ctx)
        return ok, blk

    def arrive(step):
        for i, j in stages[step]:
            ok, blk = where_from(i, j)

            @pl.when(ok)
            def _(blk=blk):
                hop(blk, 0).wait_recv()
            if j == 0:
                way = 0 if i < 0 else 1
                send(jnp.logical_and(ok, moves[way][0]), blk, way)
                send(jnp.logical_and(ok, up_b), blk, 2)
                send(jnp.logical_and(ok, dn_b), blk, 3)
            else:
                way = 2 if j < 0 else 3
                send(jnp.logical_and(ok, moves[way][0]), blk, way)
            send(ok, blk, 4)

    def settle(step):
        for i, j in stages[step]:
            ok, blk = where_from(i, j)

            @pl.when(ok)
            def _(blk=blk):
                across(blk, 1 - k).wait_recv()

    vbuf[:, :, VDIM:] = jnp.ones((heads, tok, VDIM), jnp.bfloat16)

    def attend(d):
        src = jnp.maximum(c - d, 0)
        for h in range(heads):
            part = jnp.dot(got[src, :, :, :RANK].reshape(tok, RANK),
                           w_up_ref[:, h * 256:(h + 1) * 256], preferred_element_type=jnp.float32)
            part = part.astype(jnp.bfloat16)
            kbuf[h, :, :NOPE] = part[:, :NOPE]
            kbuf[h, :, NOPE:] = got[src, :, :, RANK:].reshape(tok, ROPE)
            vbuf[h, :, :VDIM] = part[:, NOPE:]

        def head(h, carry):
            s = lax.dot_general(q_ref[h], kbuf[h], (((1,), (1,)), ((), ())),
                                preferred_element_type=jnp.float32)
            key = src * tok + lax.broadcasted_iota(jnp.int32, (tok, tok), 1)
            ok = key >= start_ref[...]
            if d == 0:
                row = c * tok + lax.broadcasted_iota(jnp.int32, (tok, tok), 0)
                ok = jnp.logical_and(ok, key <= row)
            s = jnp.where(ok, s, NEG)
            best = jnp.max(s, axis=1, keepdims=True)
            if d > 0:
                old = top[h][:, :1]
                best = jnp.maximum(old, best)
            p = jnp.exp2(s - best).astype(jnp.bfloat16)
            pv = jnp.dot(p, vbuf[h], preferred_element_type=jnp.float32)
            if d > 0:
                pv = pv + acc[h] * jnp.exp2(old - best)
            acc[h] = pv
            top[h] = jnp.broadcast_to(best, (tok, 128))
            return carry

        lax.fori_loop(0, heads, head, 0)

    def attend_if(d):
        if d <= window:
            @pl.when(c >= d)
            def _():
                attend(d)

    attend(0)
    if line_b == 2:
        arrive(1)
        settle(1)
        attend_if(2)
        arrive(2)
        settle(2)
        attend_if(1)
        attend_if(4)
        arrive(3)
        settle(3)
        attend_if(3)
        arrive(4)
    else:
        for step in range(1, far_step + 1):
            arrive(step)
            if step < far_step:
                settle(step)
        settle(far_step)
        for d in range(1, window + 1):
            attend_if(d)

    for h in range(heads):
        ho[:, h * VDIM:(h + 1) * VDIM] = (acc[h, :, :VDIM] / acc[h, :, VDIM:]).astype(jnp.bfloat16)
    rows = tok // n_head

    def project(group):
        return jnp.dot(ho[pl.ds(pl.multiple_of(group * rows, rows), rows), :], w_out_ref[...],
                       preferred_element_type=jnp.float32)

    def swap(src, dst, number, other):
        return pltpu.make_async_remote_copy(
            src_ref=src, dst_ref=dst, send_sem=sum_send.at[number], recv_sem=sum_recv.at[number],
            device_id=(c, other), device_id_type=MESH)

    turns = range(n_x - 1)
    first = [swap(sib_out.at[r], sib_in.at[r], r, sib) for r in turns]
    second = [swap(far_out.at[r], far_in.at[r], n_x + r, fars[r] * 2 + k) for r in turns]
    third = swap(near_out, near_in, n_x - 1, sib)
    fourth = swap(dsib_out, dsib_in, 2 * n_x - 1, sib)
    fifth = [swap(dfar.at[x], dfar.at[x], 2 * n_x + r, fars[r] * 2 + k) for r in turns]
    for r in turns:
        sib_out[r] = project(fars[r] * 2 + 1 - k).astype(jnp.bfloat16)
        first[r].start()
    for r in turns:
        mine = project(fars[r] * 2 + k)
        first[r].wait_recv()
        far_out[r] = (mine + sib_in[r].astype(jnp.float32)).astype(jnp.bfloat16)
        second[r].start()
    near_out[...] = project(sib).astype(jnp.bfloat16)
    third.start()
    if line_b == 2:
        settle(far_step)

    def decode(j, carry):
        best, total, mix = carry
        keys = got[j].reshape(tok, WIDTH)
        s = lax.dot_general(dq_ref[...], keys, (((1,), (1,)), ((), ())),
                            preferred_element_type=jnp.float32)
        key = j * tok + lax.broadcasted_iota(jnp.int32, s.shape, 1)
        ok = jnp.logical_and(key >= dlow_ref[...], key < dhigh_ref[...])
        s = jnp.where(ok, s, NEG)
        new = jnp.maximum(best, jnp.max(s, axis=1, keepdims=True))
        p = jnp.exp2(s - new)
        ratio = jnp.exp2(best - new)
        total = total * ratio + jnp.sum(p, axis=1, keepdims=True)
        mix = mix * ratio + jnp.dot(p.astype(jnp.bfloat16), keys[:, :RANK],
                                    preferred_element_type=jnp.float32)
        return new, total, mix

    drows = dq_ref.shape[0] // heads
    _, total, mix = lax.fori_loop(
        0, n_ctx, decode, (dtop_ref[...], jnp.ones(dtop_ref.shape, jnp.float32), dacc_ref[...]))
    mix = (mix / total).astype(jnp.bfloat16)
    dheads = [jnp.dot(mix, w_up_ref[:, h * 256 + NOPE:(h + 1) * 256],
                      preferred_element_type=jnp.float32)[h * drows:(h + 1) * drows]
              for h in range(heads)]
    dheads = jnp.concatenate(dheads, 1).astype(jnp.bfloat16)
    dsib_out[...] = jnp.dot(dheads, w_out_ref[...], preferred_element_type=jnp.float32)
    fourth.start()
    for w in range(tok // PAGE):
        blk = lax.rem(c - shift_ref[w] + n_ctx, n_ctx)
        part = got[blk, w * PAGE // half, (w * PAGE) % half:(w * PAGE) % half + PAGE, :]
        cache_ref[w * PAGE:(w + 1) * PAGE, :] = part
    fourth.wait_recv()
    dfar[x] = dsib_out[...] + dsib_in[...]
    for copy in fifth:
        copy.start()
    mine = project(m)
    third.wait_recv()
    mine = mine + near_in[...].astype(jnp.float32)
    for r in turns:
        second[r].wait_recv()
        mine = mine + far_in[r].astype(jnp.float32)
    out_ref[...] = mine.astype(jnp.bfloat16)
    for r in turns:
        source = lax.rem(x - 1 - r + n_x, n_x)
        swap(dfar.at[source], dfar.at[source], 2 * n_x + r, fars[r] * 2 + k).wait_recv()
    dec = dfar[0]
    for xo in range(1, n_x):
        dec = dec + dfar[xo]
    dec_ref[...] = dec.astype(jnp.bfloat16)
    for copy in first + second + [third, fourth] + fifth:
        copy.wait_send()
    for ok, blk, way in sent:
        @pl.when(ok)
        def _(blk=blk, way=way):
            (hop(blk, way) if way < 4 else across(blk, k)).wait_send()


def on_device(
    n_ctx, n_head, prompt_states, decode_states, lengths, page_table, w_query, w_down, kv_gain, w_up, w_out
):
    tok = prompt_states.shape[0]
    heads = w_query.shape[1] // QK
    width = w_out.shape[1]
    requests = decode_states.shape[0]
    c = lax.axis_index("ctx")
    ends = jnp.cumsum(lengths)
    starts = ends - lengths
    index = c * tok + jnp.arange(tok, dtype=jnp.int32)
    start = jnp.max(jnp.where(index[:, None] >= starts[None, :], starts[None, :], 0), 1)
    cos, sin = trig((index - start).astype(jnp.float32), ROPE)
    latent = latent_of(prompt_states, w_down, kv_gain, cos, sin)
    q = jnp.dot(prompt_states, w_query, preferred_element_type=jnp.float32)
    q = q.reshape(tok, heads, QK).transpose(1, 0, 2)
    q = (jnp.concatenate([q[..., :NOPE], turn(q[..., NOPE:], cos, sin)], -1) * SCALE).astype(
        jnp.bfloat16)

    dcos, dsin = trig(lengths.astype(jnp.float32), ROPE)
    new_key = latent_of(decode_states, w_down, kv_gain, dcos, dsin)
    dq = jnp.dot(decode_states, w_query, preferred_element_type=jnp.float32)
    dq = dq.astype(jnp.bfloat16).reshape(requests, heads, QK)
    w_key = w_up.reshape(RANK, heads, NOPE + VDIM)[:, :, :NOPE]
    dn = jnp.einsum("qhn,rhn->hqr", dq[..., :NOPE], w_key, preferred_element_type=jnp.float32)
    dr = turn(dq[..., NOPE:].astype(jnp.float32), dcos[:, None], dsin[:, None]).transpose(1, 0, 2)
    dq = (jnp.concatenate([dn, dr], -1) * SCALE).astype(jnp.bfloat16)
    own = jnp.sum(dq.astype(jnp.float32) * new_key.astype(jnp.float32)[None], -1, keepdims=True)
    per = 8 * pl.cdiv(requests, 8)
    spread = lambda v: jnp.pad(v, ((0, 0), (0, per - requests), (0, 0))).reshape(heads * per, -1)
    every = lambda v: spread(jnp.broadcast_to(v[None], (heads,) + v.shape))
    args = (
        q, latent, start[:, None], spread(dq), spread(own),
        every(new_key[:, :RANK].astype(jnp.float32)), every(starts[:, None]), every(ends[:, None]),
        page_table[:tok // PAGE] // (tok // PAGE), w_up, w_out,
    )
    vmem = pl.BlockSpec(memory_space=pltpu.VMEM)
    specs = [vmem] * len(args)
    specs[8] = pl.BlockSpec(memory_space=pltpu.SMEM)
    rows = tok // n_head
    far_count = n_head // 2 - 1
    bf = jnp.bfloat16
    out, cache, dec = pl.pallas_call(
        functools.partial(kernel, n_ctx, n_head, heads),
        out_shape=(
            jax.ShapeDtypeStruct((rows, width), bf),
            jax.ShapeDtypeStruct((tok, WIDTH), bf),
            jax.ShapeDtypeStruct((per, width), bf),
        ),
        in_specs=specs,
        out_specs=(vmem, vmem, vmem),
        scratch_shapes=[
            pltpu.VMEM((n_ctx, 2, tok // 2, WIDTH), bf),
            pltpu.VMEM((heads, tok, QK), bf),
            pltpu.VMEM((heads, tok, 2 * VDIM), bf),
            pltpu.VMEM((heads, tok, 2 * VDIM), jnp.float32),
            pltpu.VMEM((heads, tok, 128), jnp.float32),
            pltpu.VMEM((tok, heads * VDIM), bf),
        ]
        + [pltpu.VMEM((far_count, rows, width), bf)] * 4
        + [pltpu.VMEM((rows, width), bf)] * 2
        + [pltpu.VMEM((per, width), jnp.float32)] * 2
        + [pltpu.VMEM((n_head // 2, per, width), jnp.float32)]
        + [
            pltpu.SemaphoreType.DMA((5, n_ctx)),
            pltpu.SemaphoreType.DMA((n_ctx,)),
            pltpu.SemaphoreType.DMA((n_ctx,)),
            pltpu.SemaphoreType.DMA((3 * n_head // 2,)),
            pltpu.SemaphoreType.DMA((3 * n_head // 2,)),
        ],
        compiler_params=pltpu.CompilerParams(
            collective_id=0, has_side_effects=True, vmem_limit_bytes=56 * 1024 * 1024
        ),
        cost_estimate=pl.CostEstimate(
            flops=12 * 10**9, bytes_accessed=8 * 10**6, transcendentals=5 * 10**6
        ),
    )(*args)
    return out, cache, dec[:requests]


def solution(mesh):
    in_specs = (
        P("ctx", None), P(), P(), P(), P(None, "head"), P(), P(), P(None, "head"), P("head", None),
    )
    out_specs = (P(("ctx", "head"), None), P("ctx", None), P())
    return jax.shard_map(
        functools.partial(on_device, mesh.shape["ctx"], mesh.shape["head"]),
        mesh=mesh, in_specs=in_specs, out_specs=out_specs, check_vma=False,
    )
```

time: 310 us -> 107 us (0.35); the launches traced: 304 us -> 106 us
  blocking collectives: 106 us -> 0 us
  Pallas kernels: 0 us -> 66.5 us
  waiting for transfers between devices: 61.4 us -> 0 us
  matrix products: 63.2 us -> 13.9 us
  other arithmetic: 33.5 us -> 8.32 us
  between operations: 14.4 us -> 0.76 us
  starting transfers between devices: 11.5 us -> 0 us
    all_gather x3 -> x0, blocking collectives: 76.9 us -> none  [combined_all(): pieces = jax.tree.map(lambda part: lax.all_gather(part, axis), value)]
    pallas_call x0 -> x1, Pallas kernels: none -> 66.5 us  [on_device(): pl.pallas_call(functools.partial(kernel, n_ctx, n_head, heads), out_shape...]
    ppermute x3 -> x0, waiting for transfers between devices: 61.3 us -> none  [from_behind(): return lax.ppermute(block, axis, route)]
    dot_general x11 -> x3, matrix products: 56.7 us -> 6.31 us  [the longest x1 4.57 us: on_device(): q = jnp.dot(prompt_states, w_query, preferred_element_type=jnp.float32)]
    psum x1 -> x0, blocking collectives: 28.8 us -> none  [on_device(): decode_out = lax.psum(partial_out.astype(jnp.bfloat16), 'head')]
    reduce_sum x6 -> x1, other arithmetic: 16.7 us -> 0.11 us  [on_device(): jnp.sum(dq.astype(jnp.float32) * new_key.astype(jnp.float32)[None], -1, k...]
    ppermute x3 -> x0, starting transfers between devices: 11.4 us -> none  [from_behind(): return lax.ppermute(block, axis, route)]
    add x18 -> x1, other arithmetic: 6.21 us -> 0.01 us  [on_device(): index = c * tok + jnp.arange(tok, dtype=jnp.int32)]
  transfers between devices with their start and end apart: 5 -> 0, of which waited for: 3 -> 0; matrix products, arithmetic and copies ran while one was open for 14% -> 0% of each run, Pallas kernels for 0% -> 0%
where the time goes in v1:
time: 107 us; the launch traced here: 106 us
  Pallas kernels  66.5 us (62%)
  local copies, waits for them, and re-layouts  17 us (16%)
  matrix products  13.9 us (13%)
  other arithmetic  8.32 us (8%)
    pallas_call x1, Pallas kernels, on_device(): pl.pallas_call(functools.partial(kernel, n_ctx, n_head, heads), out_shape...  66.5 us
    unnamed x17, local copies, waits for them, and re-layouts  8.39 us
    dot_general x2, matrix products, latent_of(): lat = jnp.dot(states, w_down, preferred_element_type=jnp.float32)  7.57 us
    dot_general x1, matrix products, on_device(): q = jnp.dot(prompt_states, w_query, preferred_element_type=jnp.float32)  4.57 us
    reshape x1, local copies, waits for them, and re-layouts, on_device(): q = q.reshape(tok, heads, QK).transpose(1, 0, 2)  2.85 us
    another operation x3, other arithmetic  2.53 us

profile of v1, /device:TPU:17, one launch (start us, length us, event | category | flops | bytes accessed | tf_op | source)
XLA Modules:
  0.0 106.4 jit_solution(3510571617431068736)
XLA Ops:
  0.6 0.0 copy-start
  0.6 1.9 %copy-done = bf16[2048,768]{1,0:T(8,128)(2,1)S(1)} copy-done((bf16[2048,768]{1,0:T(8,128)(2,1)S(1)}, bf16[2048,768]{1,0:T(8,128)(2,1)}, u32[]{:S(2)}) %copy-start) | copy-done | bytes 3145752
  2.5 4.6 %fusion.7 = f32[512,768]{0,1:T(8,128)} fusion(bf16[512,2048]{1,0:T(8,128)(2,1)} %param.9, bf16[2048,768]{1,0:T(8,128)(2,1)S(1)} %copy-done), kind=kOutput, calls=%fused_computation.43 | convolution fusion | flops 1610612736 | bytes 6815744 | tf_op jit(solution)/shard_map/dot_general | solution.py:301
  7.1 2.9 %copy.50 = f32[512,4,192]{2,0,1:T(8,128)} copy(f32[512,4,192]{0,2,1:T(8,128)} %bitcast.27) | data formatting | bytes 3145728 | tf_op jit(solution)/shard_map/reshape | solution.py:302
  10.0 0.0 copy-start.5
  10.0 5.2 %fusion.8 = f32[512,576]{1,0:T(8,128)} fusion(bf16[512,2048]{1,0:T(8,128)(2,1)} %param.9, bf16[2048,576]{0,1:T(8,128)(2,1)} %param.14), kind=kOutput, calls=%fused_computation.44 | convolution fusion | flops 1207959552 | bytes 5636096 | tf_op jit(solution)/shard_map/dot_general | solution.py:39
  15.2 0.0 copy-done.5
  15.2 0.2 reduce-window.8
  15.3 0.1 select_reduce_fusion
  15.5 2.2 %subtract_convert_fusion = (bf16[512,32]{1,0:T(8,128)(2,1)S(1)}, bf16[512,32]{1,0:T(8,128)(2,1)S(1)}, f32[512,32]{1,0:T(8,128)S(1)}, f32[512,32]{1,0:T(8,128)S(1)}) fusion(f32[512,576]{1,0:T(8,128)} %fusion.8, f32[512]{0:T(512)S(1)} %subtract_convert_fusion.2, f32[32]{0:T(128)S(1)} %negate_power_fusion), kind=kLoop, calls=%fused_computation.13 | loop fusion | flops 147456 | bytes 329856 | tf_op jit(solution)/shard_map/convert.4
  17.7 0.0 copy-start.1
  17.7 2.0 %multiply_subtract_fusion = (f32[4,512,32]{2,1,0:T(8,128)S(1)}, f32[4,512,32]{2,1,0:T(8,128)S(1)}) fusion(f32[4,512,192]{2,1,0:T(8,128)} %bitcast.24, f32[512,32]{1,0:T(8,128)S(1)} %get-tuple-element.31, f32[512,32]{1,0:T(8,128)S(1)} %get-tuple-element.32), kind=kLoop, calls=%fused_computation.6 | loop fusion | flops 393216 | bytes 1179648 | tf_op jit(solution)/shard_map/sub | solution.py:35
  19.7 0.2 copy-done.1
  19.9 0.1 slice.77
  20.0 0.0 copy-start.2
  20.0 0.0 copy-start.4
  20.0 1.3 %fusion.q_ref = bf16[4,512,192]{2,1,0:T(8,128)(2,1)} fusion(f32[4,512,32]{2,1,0:T(8,128)S(1)} %get-tuple-element.24, f32[4,512,32]{2,1,0:T(8,128)S(1)} %get-tuple-element.23, f32[4,512,128]{2,1,0:T(8,128)S(1)} %slice.77), kind=kLoop, calls=%fused_computation.1 | loop fusion | flops 1572864 | bytes 2359296 | tf_op jit(solution)/shard_map/convert_element_type | solution.py:303
  21.3 0.0 copy-done.2
  21.3 0.0 copy-start.3
  21.3 0.1 multiply_reduce_fusion
  21.5 0.0 copy-done.4
  21.5 0.2 multiply_convert_fusion
  21.7 1.0 pad_maximum_fusion.lat_ref
  22.6 0.9 copy.59.start_ref
  23.5 0.0 copy-done.3
  23.5 2.4 %fusion.9 = f32[4,576]{1,0:T(4,128)S(1)} fusion(bf16[4,2048]{1,0:T(4,128)(2,1)S(1)} %copy-done.3, bf16[2048,576]{0,1:T(8,128)(2,1)} %param.14), kind=kOutput, calls=%fused_computation.45 | convolution fusion | flops 9437184 | bytes 2384896 | tf_op jit(solution)/shard_map/dot_general | solution.py:39
  25.8 0.1 multiply_cosine_fusion.1
  26.0 0.1 multiply_reduce_fusion.2
  26.1 0.1 multiply_convert_fusion.1
  26.2 0.1 maximum_convert_fusion
  26.3 0.5 convolution_convert_fusion
  26.8 0.1 reshape.221
  26.9 0.1 multiply_subtract_fusion.1
  27.0 0.1 maximum_bitcast_fusion
  27.1 2.3 %copy.56 = bf16[512,1024]{0,1:T(8,128)(2,1)} copy(bf16[512,1024]{1,0:T(8,128)(2,1)} %w_up_ref.1) | data formatting | bytes 2097152 | tf_op args[7]
  29.4 1.2 %fusion.1 = f32[4,4,512]{2,1,0:T(4,128)S(1)} fusion(bf16[512,4,256]{0,2,1:T(8,128)(2,1)} %bitcast.26, bf16[4,4,128]{2,1,0:T(4,128)(2,1)S(1)} %slice.83), kind=kOutput, calls=%fused_computation.8 | convolution fusion | flops 2097152 | bytes 561152 | tf_op jit(solution)/shard_map/qhn,rhn->hqr/dot_general | solution.py:311
  30.6 0.1 multiply_reduce_fusion.1
  30.7 0.6 pad_bitcast_fusion.1.dq_ref
  31.3 0.7 reshape.226.dtop_ref
  32.0 0.6 pad_bitcast_fusion.dacc_ref
  32.7 0.7 pad.36.dlow_ref
  33.3 0.7 pad.37.dhigh_ref
  34.0 0.0 copy-done.6
  34.0 0.5 and_select_fusion.shift_ref
  34.6 66.5 %shard_map.112 = (bf16[128,2048]{1,0:T(8,128)(2,1)}, bf16[512,576]{1,0:T(8,128)(2,1)}, bf16[8,2048]{1,0:T(8,128)(2,1)}) custom-call(bf16[4,512,192]{2,1,0:T(8,128)(2,1)} %fusion.q_ref, bf16[512,576]{1,0:T(8,128)(2,1)} %pad_maximum_fusion.lat_ref, s32[512,1]{1,0:T(8,128)} %copy.59.start_ref, bf16[32,576]{1,0:T(8,128)(2,1)} %pad_bitcast_fusion.1.dq_ref, ...), custom_call_target="tpu_custom_call" | custom-call | flops 12000000000 | bytes 8000000 | tf_op jit(solution)/shard_map/pallas_call | solution.py:329
  101.1 2.1 %copy.63 = bf16[512,576]{0,1:T(8,128)(2,1)} copy(bf16[512,576]{1,0:T(8,128)(2,1)} %get-tuple-element.19) | data formatting | bytes 1179648
  103.2 1.4 %slice.76 = bf16[4,2048]{1,0:T(4,128)(2,1)} slice(bf16[8,2048]{1,0:T(8,128)(2,1)} %get-tuple-element.8), slice={[0:4], [0:2048]} | slice | bytes 32768 | tf_op jit(solution)/shard_map/slice | solution.py:364
  104.6 1.9 %copy.73 = bf16[128,2048]{1,0:T(8,128)(2,1)} copy(bf16[128,2048]{1,0:T(8,128)(2,1)} %get-tuple-element.42) | data formatting | bytes 1048576
  (16 shorter events, 0.1 us)
Async XLA Ops:
  0.6 1.9 %copy-start = (bf16[2048,768]{1,0:T(8,128)(2,1)S(1)}, bf16[2048,768]{1,0:T(8,128)(2,1)}, u32[]{:S(2)}) copy-start(bf16[2048,768]{1,0:T(8,128)(2,1)} %param.13) | copy-start | bytes 9437188
  10.0 5.2 %copy-start.5 = (s32[4]{0:T(128)S(1)}, s32[4]{0:T(128)}, u32[]{:S(2)}) copy-start(s32[4]{0:T(128)} %param.11) | copy-start | bytes 52
  17.7 2.2 %copy-start.1 = (f32[512,4,192]{2,0,1:T(8,128)S(1)}, f32[512,4,192]{2,0,1:T(8,128)}, u32[]{:S(2)}) copy-start(f32[512,4,192]{2,0,1:T(8,128)} %copy.50) | copy-start | bytes 4718596
  20.0 1.4 %copy-start.2 = (f32[512,576]{1,0:T(8,128)S(1)}, f32[512,576]{1,0:T(8,128)}, u32[]{:S(2)}) copy-start(f32[512,576]{1,0:T(8,128)} %fusion.8) | copy-start | bytes 3538948
  20.0 1.5 %copy-start.4 = (f32[512]{0:T(512)S(1)}, f32[512]{0:T(512)}, u32[]{:S(2)}) copy-start(f32[512]{0:T(512)} %param.15) | copy-start | bytes 6148
  21.3 2.1 %copy-start.3 = (bf16[4,2048]{1,0:T(4,128)(2,1)S(1)}, bf16[4,2048]{1,0:T(4,128)(2,1)}, u32[]{:S(2)}) copy-start(bf16[4,2048]{1,0:T(4,128)(2,1)} %param.10) | copy-start | bytes 49156
  26.8 7.3 %copy-start.6 = (s32[32]{0:T(128)S(1)}, s32[32]{0:T(128)}, u32[]{:S(2)}) copy-start(s32[32]{0:T(128)} %param.12) | copy-start | bytes 388
